TPU v7x, 128 devices: a whole 4x4x4 slice. The times are simulated.
128 devices in a mesh: outer: 8 (over z, x_hi), inner: 16 (over y, x_lo, core).
Axes of the slice: x: 4 (x_hi: 2, x_lo: 2; x = x_hi * 2 + x_lo), y: 4, z: 4, core: 2. Of those that a mesh axis runs over, the one named last changes fastest.
Arguments:
- queries: bfloat16 [16384, 3072], P(('outer', 'inner')), may hold values from -16 to 16
- keys: bfloat16 [16384, 512], P(('outer', 'inner')), may hold values from -16 to 16
- values: bfloat16 [16384, 512], P(('outer', 'inner')), may hold values from -6 to 6
- output_gradient: bfloat16 [16384, 3072], P(('outer', 'inner')), may hold values from -6 to 6
- span_order: int32 [32], replicated, may hold values from 0 to 31, each once
Outputs:
- grad_queries: bfloat16 [16384, 3072], P(('outer', 'inner'))
- key_gradients_out: bfloat16 [16384, 512], P(('outer', 'inner'))
- value_gradients_out: bfloat16 [16384, 512], P(('outer', 'inner'))
Inputs may be any that keep to these rules, and one draw needn't show every extreme that they name: `span_order`: each of 0 to 31 once.
All inputs are finite; a program needn't handle non-finite values.
Results may differ from a plain program's by a relative error of at most 0.04.
Values may be sent and summed in bfloat16 or wider, within the bound.
A program may use at most 128 MiB of HBM per device.

v0:
```python
import math

import jax
import jax.numpy as jnp
from jax import lax
from jax.sharding import PartitionSpec as P

HEAD_SIZE = 128


masked_score = -1e30


def from_behind(value, axis, steps):
    count = lax.axis_size(axis)
    first, last = (max(0, -steps), min(count, count - steps))
    return lax.ppermute(value, axis, [(source, source + steps) for source in range(first, last)])


def on_device(queries, keys, values, output_gradient, span_order):
    tok_rows = queries.shape[0]
    half_len = tok_rows // 2
    group_len = tok_rows * lax.axis_size("inner")
    heads_kv = keys.shape[1] // HEAD_SIZE
    group_size = queries.shape[1] // (heads_kv * HEAD_SIZE)
    scale = HEAD_SIZE ** (-0.5)
    outer_idx = lax.axis_index("outer")
    inner_idx = lax.axis_index("inner")
    span_count = span_order.shape[0]
    span_ids = jnp.arange(span_count, dtype=jnp.int32)

    def lookup(indices):
        return jnp.sum(
            jnp.where(indices[:, None] == span_ids[None, :], span_order[None, :], 0), axis=1
        )

    local_rows = inner_idx * tok_rows + jnp.arange(tok_rows, dtype=jnp.int32)
    query_pos = lookup(local_rows // half_len) * half_len + local_rows % half_len
    rows_of_keys = jnp.arange(group_len, dtype=jnp.int32)
    own_pos = lookup(rows_of_keys // half_len) * half_len + rows_of_keys % half_len
    key_pos = jnp.concatenate([jnp.zeros((group_len,), jnp.int32), own_pos])
    from_prev = jnp.arange(2 * group_len, dtype=jnp.int32) < group_len
    has_prev = outer_idx > 0
    earlier_keys, earlier_values = from_behind((keys, values), "outer", 1)
    gathered = (
        lax.all_gather(earlier_keys, "inner", axis=0, tiled=True),
        lax.all_gather(earlier_values, "inner", axis=0, tiled=True),
        lax.all_gather(keys, "inner", axis=0, tiled=True),
        lax.all_gather(values, "inner", axis=0, tiled=True),
    )
    stacked_keys = jnp.concatenate([gathered[0], gathered[2]], axis=0)
    stacked_values = jnp.concatenate([gathered[1], gathered[3]], axis=0)
    total_keys = 2 * group_len
    block_len = math.gcd(total_keys, 512)
    block_count = total_keys // block_len
    query_transposed = queries.reshape(tok_rows, heads_kv, group_size, HEAD_SIZE).transpose(
        1, 2, 0, 3
    )
    gradient_transposed = output_gradient.reshape(
        tok_rows, heads_kv, group_size, HEAD_SIZE
    ).transpose(1, 2, 0, 3)

    def block_scores(block_idx):
        start = block_idx * block_len
        block_of_keys = lax.dynamic_slice_in_dim(stacked_keys, start, block_len, 0).reshape(
            block_len, heads_kv, HEAD_SIZE
        )
        block_of_values = lax.dynamic_slice_in_dim(stacked_values, start, block_len, 0).reshape(
            block_len, heads_kv, HEAD_SIZE
        )
        pos_block = lax.dynamic_slice_in_dim(key_pos, start, block_len, 0)
        prev_block = lax.dynamic_slice_in_dim(from_prev, start, block_len, 0)
        visible = jnp.where(prev_block[None, :], has_prev, pos_block[None, :] <= query_pos[:, None])
        scores = (
            jnp.einsum(
                "hoxz,qhz->hoxq",
                query_transposed,
                block_of_keys,
                preferred_element_type=jnp.float32,
            )
            * scale
        )
        return (jnp.where(visible, scores, masked_score), visible, block_of_keys, block_of_values)

    def stats_step(block_idx, totals):
        running_max, running_sum = totals
        scores, visible, block_of_keys, block_of_values = block_scores(block_idx)
        new_max = jnp.maximum(running_max, jnp.max(scores, axis=-1))
        fresh = jnp.sum(jnp.where(visible, jnp.exp(scores - new_max[..., None]), 0.0), axis=-1)
        return (new_max, running_sum * jnp.exp(running_max - new_max) + fresh)

    stat_shape = (heads_kv, group_size, tok_rows)
    running_max, running_sum = lax.fori_loop(
        0,
        block_count,
        stats_step,
        (jnp.full(stat_shape, masked_score, jnp.float32), jnp.zeros(stat_shape, jnp.float32)),
    )
    log_total = running_max + jnp.log(running_sum)

    def value_step(block_idx, totals):
        out_acc, dv_terms = totals
        scores, visible, block_of_keys, block_of_values = block_scores(block_idx)
        probabilities = jnp.where(visible, jnp.exp(scores - log_total[..., None]), 0.0).astype(
            jnp.bfloat16
        )
        out_acc = out_acc + jnp.einsum(
            "twoi,ity->twoy", probabilities, block_of_values, preferred_element_type=jnp.float32
        )
        dv_block = jnp.einsum(
            "ntgy,ntgr->ynr", probabilities, gradient_transposed, preferred_element_type=jnp.float32
        ).reshape(block_len, heads_kv * HEAD_SIZE)
        return (
            out_acc,
            lax.dynamic_update_slice_in_dim(dv_terms, dv_block, block_idx * block_len, 0),
        )

    out_acc, dv_terms = lax.fori_loop(
        0,
        block_count,
        value_step,
        (
            jnp.zeros((heads_kv, group_size, tok_rows, HEAD_SIZE), jnp.float32),
            jnp.zeros((total_keys, heads_kv * HEAD_SIZE), jnp.float32),
        ),
    )
    output = out_acc.astype(jnp.bfloat16)
    delta = jnp.sum(gradient_transposed.astype(jnp.float32) * output.astype(jnp.float32), axis=-1)

    def grad_step(block_idx, totals):
        dq_acc, dk_terms = totals
        scores, visible, block_of_keys, block_of_values = block_scores(block_idx)
        probabilities = jnp.where(visible, jnp.exp(scores - log_total[..., None]), 0.0)
        dprobs = jnp.einsum(
            "hoxz,qhz->hoxq",
            gradient_transposed,
            block_of_values,
            preferred_element_type=jnp.float32,
        )
        score_gradient = (probabilities * (dprobs - delta[..., None])).astype(jnp.bfloat16)
        dq_acc = dq_acc + jnp.einsum(
            "twoi,ity->twoy", score_gradient, block_of_keys, preferred_element_type=jnp.float32
        )
        dk_block = (
            jnp.einsum(
                "ntgy,ntgr->ynr",
                score_gradient,
                query_transposed,
                preferred_element_type=jnp.float32,
            )
            * scale
        ).reshape(block_len, heads_kv * HEAD_SIZE)
        return (
            dq_acc,
            lax.dynamic_update_slice_in_dim(dk_terms, dk_block, block_idx * block_len, 0),
        )

    dq_acc, dk_terms = lax.fori_loop(
        0,
        block_count,
        grad_step,
        (
            jnp.zeros((heads_kv, group_size, tok_rows, HEAD_SIZE), jnp.float32),
            jnp.zeros((total_keys, heads_kv * HEAD_SIZE), jnp.float32),
        ),
    )
    grad_queries = (
        (dq_acc * scale)
        .transpose(2, 0, 1, 3)
        .reshape(tok_rows, heads_kv * group_size * HEAD_SIZE)
        .astype(jnp.bfloat16)
    )
    summed = (
        lax.psum_scatter(
            dk_terms[:group_len].astype(jnp.bfloat16), "inner", scatter_dimension=0, tiled=True
        ).astype(jnp.float32),
        lax.psum_scatter(
            dv_terms[:group_len].astype(jnp.bfloat16), "inner", scatter_dimension=0, tiled=True
        ).astype(jnp.float32),
        lax.psum_scatter(
            dk_terms[group_len:].astype(jnp.bfloat16), "inner", scatter_dimension=0, tiled=True
        ).astype(jnp.float32),
        lax.psum_scatter(
            dv_terms[group_len:].astype(jnp.bfloat16), "inner", scatter_dimension=0, tiled=True
        ).astype(jnp.float32),
    )
    returned = (
        from_behind(summed[0].astype(jnp.bfloat16), "outer", -1).astype(jnp.float32),
        from_behind(summed[1].astype(jnp.bfloat16), "outer", -1).astype(jnp.float32),
    )
    key_gradients_out = summed[2] + returned[0]
    value_gradients_out = summed[3] + returned[1]
    return (
        grad_queries,
        key_gradients_out.astype(jnp.bfloat16),
        value_gradients_out.astype(jnp.bfloat16),
    )


def solution(mesh):
    return jax.shard_map(
        on_device,
        mesh=mesh,
        in_specs=(
            P(("outer", "inner"), None),
            P(("outer", "inner"), None),
            P(("outer", "inner"), None),
            P(("outer", "inner"), None),
            P(),
        ),
        out_specs=(
            P(("outer", "inner"), None),
            P(("outer", "inner"), None),
            P(("outer", "inner"), None),
        ),
        check_vma=False,
    )
```

profile of v0, /device:TPU:34, one launch (start us, length us, event | category | flops | bytes accessed | tf_op | source)
XLA Modules:
  0.0 657.3 jit_solution(4831791859974737019)
XLA Ops:
  12.4 5.5 collective-permute-done
  23.5 6.1 collective-permute-done.1
  38.1 18.6 %all-gather.5.cloned.1.call-done = bf16[2048,512]{0,1:T(8,128)(2,1)} async-done(((bf16[128,512]{0,1:T(8,128)(2,1)}), bf16[2048,512]{0,1:T(8,128)(2,1)}) %all-gather.5.cloned.1.call-update) | async-done | bytes 2097168 | tf_op jit(solution)/shard_map/all_gather | solution.py:46
  60.0 36.5 %all-gather.7.cloned.1.call-done = bf16[2048,512]{0,1:T(8,128)(2,1)} async-done(((bf16[128,512]{0,1:T(8,128)(2,1)}), bf16[2048,512]{0,1:T(8,128)(2,1)}) %all-gather.7.cloned.1.call-update) | async-done | bytes 2097168 | tf_op jit(solution)/shard_map/all_gather | solution.py:48
  99.7 85.5 %while.48 = (s32[]{:T(128)}, f32[4,6,128]{2,1,0:T(8,128)S(1)}, f32[4,6,128]{2,1,0:T(8,128)S(1)}, pred[4096]{0:T(1024)(128)(4,1)S(1)}, pred[]{:T(512)}, /*index=5...) while((s32[]{:T(128)}, f32[4,6,128]{2,1,0:T(8,128)S(1)}, ...), condition=%wide.region_5.6_spmd.clone, body=%wide.region_2.5_spmd.clone.sunk | while | flops 415382528 | bytes 15306947 | solution.py:93
  101.1 4.8 fusion.65
  106.0 4.4 select_reduce_fusion.4
  111.9 4.9 fusion.65
  122.5 4.9 fusion.65
  127.4 4.3 select_reduce_fusion.4
  133.2 4.8 fusion.65
  143.9 4.9 fusion.65
  148.7 4.3 select_reduce_fusion.4
  154.6 4.9 fusion.65
  165.3 4.8 fusion.65
  170.1 4.3 select_reduce_fusion.4
  176.0 4.8 fusion.65
  193.8 131.1 %while.49 = (s32[]{:T(128)}, f32[4,6,128,128]{3,2,1,0:T(8,128)}, bf16[4096,512]{1,0:T(8,128)(2,1)}, pred[4096]{0:T(1024)(128)(4,1)S(1)}, pred[]{:T(512)}, /*inde...) while((s32[]{:T(128)}, f32[4,6,128,128]{3,2,1,0:T(8,128)}, ...), condition=%wide.region_7.8_spmd.clone, body=%wide.region_6.7_spmd.clone.sunk | while | flops 1216741376 | bytes 20074716 | solution.py:118
  324.9 4.6 fusion.20
  334.9 117.1 %while.50 = (s32[]{:T(128)}, f32[4,6,128,128]{3,2,1,0:T(8,128)S(1)}, bf16[4096,512]{1,0:T(8,128)(2,1)}, pred[4096]{0:T(1024)(128)(4,1)S(1)}, pred[]{:T(512)}, /*...) while((s32[]{:T(128)}, ...), condition=%wide.region_10.11_spmd.clone, body=%wide.region_9.10_spmd.clone.sunk | while | flops 1623064576 | bytes 49709340 | solution.py:158
  452.0 4.5 fusion.21
  464.0 53.9 %reduce-scatter.7.cloned.1.call-done = bf16[128,512]{1,0:T(8,128)(2,1)} async-done(((bf16[2048,512]{1,0:T(8,128)(2,1)}), bf16[128,512]{1,0:T(8,128)(2,1)}) %reduce-scatter.7.cloned.1.call-update) | async-done | bytes 131088 | tf_op jit(solution)/shard_map/reduce_scatter | solution.py:174
  521.3 61.9 %reduce-scatter.9.cloned.1.call-done = bf16[128,512]{1,0:T(8,128)(2,1)} async-done(((bf16[2048,512]{1,0:T(8,128)(2,1)}), bf16[128,512]{1,0:T(8,128)(2,1)}) %reduce-scatter.9.cloned.1.call-update) | async-done | bytes 131088 | tf_op jit(solution)/shard_map/reduce_scatter | solution.py:183
  584.8 64.1 %reduce-scatter.5.cloned.1.call-done = bf16[128,512]{1,0:T(8,128)(2,1)} async-done(((bf16[2048,512]{1,0:T(8,128)(2,1)}), bf16[128,512]{1,0:T(8,128)(2,1)}) %reduce-scatter.5.cloned.1.call-update) | async-done | bytes 131088 | tf_op jit(solution)/shard_map/reduce_scatter | solution.py:180
  (321 shorter events, 330.0 us)
Async XLA Ops:
  7.2 27.3 %copy-start.11 = (s32[32]{0:T(128)S(1)}, s32[32]{0:T(128)}, u32[]{:S(2)}) copy-start(s32[32]{0:T(128)} %param.15) | copy-start | bytes 388
  7.2 27.5 %copy-start.5 = (bf16[128,3072]{1,0:T(8,128)(2,1)S(1)}, bf16[128,3072]{1,0:T(8,128)(2,1)}, u32[]{:S(2)}) copy-start(bf16[128,3072]{1,0:T(8,128)(2,1)} %param.14) | copy-start | bytes 2359300
  7.2 49.6 %all-gather.5.cloned.1.call-start = ((), (), s32[]{:S(2)}) async-start(), calls=%async_computation.4 | async-start | bytes 2228224 | tf_op jit(solution)/shard_map/all_gather | solution.py:46
  8.3 10.3 %copy-start.8 = (bf16[128,512]{0,1:T(8,128)(2,1)}, bf16[128,512]{0,1:T(8,128)(2,1)S(1)}, u32[]{:S(2)}) copy-start(bf16[128,512]{0,1:T(8,128)(2,1)S(1)} %copy.56) | copy-start | bytes 393220
  8.3 9.5 %collective-permute-start = (bf16[128,512]{0,1:T(8,128)(2,1)S(1)}, bf16[128,512]{0,1:T(8,128)(2,1)S(1)}, u32[]{:S(2)}, u32[]{:S(2)}) collective-permute-start(bf16[128,512]{0,1:T(8,128)(2,1)S(1)} %copy.56), channel_id=1, source_target_pairs={{0,16},{16,32},{32,48},{48,64},{64,80},{80,96},{96,112},{1,17},{17... | collective-permute-start | bytes 393224 | tf_op jit(solution)/shard_map/ppermute | solution.py:17
  18.6 77.9 %all-gather.7.cloned.1.call-start = ((), (), s32[]{:S(2)}) async-start(), calls=%async_computation.5 | async-start | bytes 2228224 | tf_op jit(solution)/shard_map/all_gather | solution.py:48
  19.3 165.9 %all-gather.9.cloned.1.call-start = ((), (), s32[]{:S(2)}) async-start(), calls=%async_computation.6 | async-start | bytes 2228224 | tf_op jit(solution)/shard_map/all_gather | solution.py:47
  20.4 10.0 %copy-start.7 = (bf16[128,512]{0,1:T(8,128)(2,1)}, bf16[128,512]{0,1:T(8,128)(2,1)S(1)}, u32[]{:S(2)}) copy-start(bf16[128,512]{0,1:T(8,128)(2,1)S(1)} %copy.60) | copy-start | bytes 393220
  20.4 9.3 %collective-permute-start.1 = (bf16[128,512]{0,1:T(8,128)(2,1)S(1)}, bf16[128,512]{0,1:T(8,128)(2,1)S(1)}, u32[]{:S(2)}, u32[]{:S(2)}) collective-permute-start(bf16[128,512]{0,1:T(8,128)(2,1)S(1)} %copy.60), channel_id=1, source_target_pairs={{0,16},{16,32},{32,48},{48,64},{64,80},{80,96},{96,112},{1,17},{17... | collective-permute-start | bytes 393224 | tf_op jit(solution)/shard_map/ppermute | solution.py:17
  30.3 158.0 %all-gather.11.cloned.1.call-start = ((), (), s32[]{:S(2)}) async-start(), calls=%async_computation.7 | async-start | bytes 2228224 | tf_op jit(solution)/shard_map/all_gather | solution.py:49
  30.9 427.6 %reduce-scatter.11.cloned.1.call-start = ((), (), s32[]{:S(2)}) async-start(), calls=%async_computation.11 | async-start | bytes 2228224 | tf_op jit(solution)/shard_map/reduce_scatter | solution.py:177
  33.3 26.6 %copy-start.3 = (bf16[128,3072]{0,1:T(8,128)(2,1)}, bf16[128,3072]{0,1:T(8,128)(2,1)S(1)}, u32[]{:S(2)}) copy-start(bf16[128,3072]{0,1:T(8,128)(2,1)S(1)} %copy.58) | copy-start | bytes 2359300
  324.9 4.8 copy-start.2
  329.5 5.4 copy-start.1
  329.5 188.3 %reduce-scatter.7.cloned.1.call-start = ((), (), s32[]{:S(2)}) async-start(), calls=%async_computation.9 | async-start | bytes 2228224 | tf_op jit(solution)/shard_map/reduce_scatter | solution.py:174
  330.9 4.0 copy-start.4
  340.3 1.7 copy-start
  354.9 1.7 copy-start
  369.6 1.7 copy-start
  428.1 1.7 copy-start
  456.5 126.7 %reduce-scatter.9.cloned.1.call-start = ((), (), s32[]{:S(2)}) async-start(), calls=%async_computation.10 | async-start | bytes 2228224 | tf_op jit(solution)/shard_map/reduce_scatter | solution.py:183
  457.3 191.6 %reduce-scatter.5.cloned.1.call-start = ((), (), s32[]{:S(2)}) async-start(), calls=%async_computation.8 | async-start | bytes 2228224 | tf_op jit(solution)/shard_map/reduce_scatter | solution.py:180
  458.5 124.7 %collective-permute-start.3 = (bf16[128,512]{1,0:T(8,128)(2,1)}, bf16[128,512]{1,0:T(8,128)(2,1)S(1)}, u32[]{:S(2)}, u32[]{:S(2)}) collective-permute-start(bf16[128,512]{1,0:T(8,128)(2,1)} %reduce-scatter.11.cloned.1.call-done), channel_id=1, source_target_pairs={{16,0},{32,16},{48,32},{64,48},{80,64},{96,80},{112,96},{17,1},{33... | collective-permute-start | bytes 393224 | tf_op jit(solution)/shard_map/ppermute | solution.py:17
  517.9 131.0 %collective-permute-start.2 = (bf16[128,512]{1,0:T(8,128)(2,1)}, bf16[128,512]{1,0:T(8,128)(2,1)S(1)}, u32[]{:S(2)}, u32[]{:S(2)}) collective-permute-start(bf16[128,512]{1,0:T(8,128)(2,1)} %reduce-scatter.7.cloned.1.call-done), channel_id=1, source_target_pairs={{16,0},{32,16},{48,32},{64,48},{80,64},{96,80},{112,96},{17,1},{33... | collective-permute-start | bytes 393224 | tf_op jit(solution)/shard_map/ppermute | solution.py:17
  (14 other events, 17.1 us)
Sparse Core Ops, SparseCore 0:
  18.7 38.0 all-gather.4
  58.9 37.4 all-gather.6
  98.1 37.4 all-gather.8
  137.1 37.4 all-gather.10
  329.6 61.2 reduce-scatter.10
  456.6 61.1 reduce-scatter.6
  520.3 62.9 reduce-scatter.8
  585.6 63.2 reduce-scatter.4
where the time goes:
time: 666 us; the launch traced here: 657 us
  waiting for transfers between devices  249 us (37%)
  matrix products  192 us (29%)
  local copies, waits for them, and re-layouts  140 us (21%)
  other arithmetic  45.6 us (7%)
  starting transfers between devices  15.1 us (2%)
  between operations  14.4 us (2%)
    dot_general x24, matrix products, block_scores(): jnp.einsum('hoxz,qhz->hoxq', query_transposed, block_of_keys, preferred_e...  71.9 us
    reduce_scatter x1, waiting for transfers between devices, on_device(): lax.psum_scatter(dk_terms[group_len:].astype(jnp.bfloat16), 'inner', scat...  64.1 us
    reduce_scatter x1, waiting for transfers between devices, on_device(): lax.psum_scatter(dv_terms[group_len:].astype(jnp.bfloat16), 'inner', scat...  61.9 us
    reduce_scatter x1, waiting for transfers between devices, on_device(): lax.psum_scatter(dk_terms[:group_len].astype(jnp.bfloat16), 'inner', scat...  53.9 us
    all_gather x1, waiting for transfers between devices, on_device(): lax.all_gather(keys, 'inner', axis=0, tiled=True)  36.5 us
    reduce_sum x8, other arithmetic, stats_step(): jnp.sum(jnp.where(visible, jnp.exp(scores - new_max[..., None]), 0.0), ax...  34.5 us
    dynamic_update_slice x16, local copies, waits for them, and re-layouts, value_step(): lax.dynamic_update_slice_in_dim(dv_terms, dv_block, block_idx * block_len...  31.5 us
    dot_general x8, matrix products, value_step(): jnp.einsum('twoi,ity->twoy', probabilities, block_of_values, preferred_el...  30.7 us
  transfers between devices with their start and end apart: 12, of which 7 were waited for; matrix products, arithmetic and copies ran while one was open for 33% of the time, Pallas kernels for 0%

commit v1 on v0

v1 whole, which is shorter than its diff:
```python
import jax
import jax.numpy as jnp
from jax import lax
from jax.experimental import pallas as pl
from jax.experimental.pallas import tpu as pltpu
from jax.sharding import PartitionSpec as P

MESH = pl.DeviceIdType.MESH
F32 = jnp.float32
BF16 = jnp.bfloat16
SCALE = 128**-0.5
SCALE2 = SCALE * 1.4426950408889634
MASKED = -1.0e30
NT = (((1,), (1,)), ((), ()))

HEAD = 128
TOK = 128
NH = 3
SET = 2 * TOK
ROWS = NH * SET
COLS = NH * HEAD
SEG = 8 * TOK
NKEY = 4 * SEG
BK = SEG
VR = 16


def kernel(
    q_ref, k_ref, v_ref, do_ref, span_ref,
    gq_ref, gk_ref, gv_ref,
    qraw, doraw, kvg, pk, pq, qt, dot, s_buf, dp_buf, e_buf, mx, ls, dd, dqa, dka, dva, dqs,
    cx, rx, xs, xr, ys, yr,
    q_ssem, q_rsem, y_ssem, y_rsem, x_ssem, x_rsem, c_ssem, c_rsem, l_sem,
    dq_ssem, dq_rsem, rc_ssem, rc_rsem, rx_ssem, rx_rsem, ry_ssem, ry_rsem,
):
    o = lax.axis_index("outer")
    i = lax.axis_index("inner")
    y, xl, c = i // 4, (i // 2) % 2, i % 2
    has_prev = o > 0
    has_next = o < 7

    def dev(oo, yy, xx, cc):
        return (oo, yy * 4 + xx * 2 + cc)

    def yrel(d):
        return lax.rem(y + d, 4)

    def remote(src, dst, ssem, rsem, device):
        return pltpu.make_async_remote_copy(
            src_ref=src, dst_ref=dst, send_sem=ssem, recv_sem=rsem, device_id=device, device_id_type=MESH
        )

    o_next, o_prev = lax.rem(o + 1, 8), lax.rem(o + 7, 8)
    core = dev(o, y, xl, 1 - c)

    barrier = pltpu.get_barrier_semaphore()
    peers = [dev(o, yrel(d), xl, cc) for d in range(1, 4) for cc in range(2)]
    peers += [core, dev(o, y, 1 - xl, c)]
    peers += [dev(oo, y, xx, c) for oo in (o_next, o_prev) for xx in range(2)]
    for p in peers:
        pl.semaphore_signal(barrier, inc=1, device_id=p, device_id_type=MESH)
    pl.semaphore_wait(barrier, len(peers))

    def rows(seg, cc, yy=0, n=4):
        return pl.ds(pl.multiple_of(seg * SEG + cc * 4 * TOK + yy * TOK, TOK), n * TOK)

    def kv_copy(t, d):
        yy = yrel(d)
        src = (k_ref, v_ref)[t].at[:, pl.ds(pl.multiple_of(yy * HEAD, HEAD), HEAD)]
        return remote(src, kvg.at[t, rows(0, c, y, 1)], y_ssem.at[t, d - 1], y_rsem.at[t, 3 - d], dev(o, yy, xl, c))

    def kv_local(t):
        src = (k_ref, v_ref)[t].at[:, pl.ds(pl.multiple_of(y * HEAD, HEAD), HEAD)]
        return pltpu.make_async_copy(src, kvg.at[t, rows(0, c, y, 1)], l_sem.at[t])

    def q_copy(t, d, dc):
        yy, cc = yrel(d), (1 - c if dc else c)
        src = (q_ref, do_ref)[t].at[:, pl.ds(pl.multiple_of((yy * 2 + cc) * COLS, 128), COLS)]
        dst = (qraw, doraw)[t].at[(4 - d) % 4, pl.ds(pl.multiple_of(c * TOK, TOK), TOK)]
        r = (4 - d) % 4
        return remote(src, dst, q_ssem.at[t, d, dc], q_rsem.at[t, r, dc], dev(o, yy, xl, cc))

    def q_local(t):
        src = (q_ref, do_ref)[t].at[:, pl.ds(pl.multiple_of((y * 2 + c) * COLS, 128), COLS)]
        dst = (qraw, doraw)[t].at[0, pl.ds(pl.multiple_of(c * TOK, TOK), TOK)]
        return pltpu.make_async_copy(src, dst, l_sem.at[2 + t])

    def x_copy(n):
        src = kvg.at[:, rows(0, c)]
        if n == 0:
            return remote(src, kvg.at[:, rows(1, c)], x_ssem.at[0], x_rsem.at[0], dev(o, y, 1 - xl, c))
        return remote(src, kvg.at[:, rows(2 + xl, c)], x_ssem.at[n], x_rsem.at[1 + xl], dev(o_next, y, n - 1, c))

    def x_arrival(n):
        dst = kvg.at[:, rows(1 + n, c)]
        return remote(dst, dst, x_ssem.at[0], x_rsem.at[n], core)

    def c_copy(seg):
        blk = kvg.at[:, rows(seg, c)]
        return remote(blk, blk, c_ssem.at[seg], c_rsem.at[seg], core)

    def c_arrival(seg):
        blk = kvg.at[:, rows(seg, 1 - c)]
        return remote(blk, blk, c_ssem.at[seg], c_rsem.at[seg], core)

    for t in range(2):
        kv_local(t).start()
        q_local(t).start()
        for d in range(1, 4):
            kv_copy(t, d).start()
    for d in (0, 3, 1, 2):
        for dc in range(2):
            for t in range(2):
                if d or dc:
                    q_copy(t, d, dc).start()

    def pk_row(blk, value):
        pk[:, pl.ds(pl.multiple_of(blk * TOK, TOK), TOK)] = value

    lane = lax.broadcasted_iota(jnp.int32, (8, TOK), 1)
    for xx in range(2):
        for cc in range(2):
            for yy in range(4):
                first = 2 * (yy * 4 + xx * 2 + cc)
                span = jnp.where(lane < 64, span_ref[first], span_ref[first + 1])
                blk = jnp.where(xl == xx, 0, 8) + cc * 4 + yy
                pk_row(blk, (span * 64 + lax.rem(lane, 64)).astype(F32))
    for blk in range(16, 32):
        pk_row(blk, jnp.full((8, TOK), -1.0, F32))
    sub = lax.broadcasted_iota(jnp.int32, (64, 128), 0)
    for rel in range(4):
        for cc in range(2):
            for hb in range(2):
                span = span_ref[2 * (yrel(rel) * 4 + xl * 2 + cc) + hb]
                at = (cc * 2 + hb) * 64
                pq[rel, at : at + 64, :] = (span * 64 + sub).astype(F32)

    dka[...] = jnp.zeros_like(dka)
    dva[...] = jnp.zeros_like(dva)

    for t in range(2):
        kv_local(t).wait()
        for d in range(1, 4):
            kv_copy(t, d).wait_recv()
    x_copy(0).start()

    @pl.when(has_next)
    def _():
        x_copy(1).start()
        x_copy(2).start()

    c_copy(0).start()
    c_arrival(0).wait_recv()
    x_arrival(0).wait_recv()
    c_copy(1).start()

    @pl.when(has_prev)
    def _():
        for n in (1, 2):
            x_arrival(n).wait_recv()
            c_copy(1 + n).start()

    c_arrival(1).wait_recv()

    @pl.when(has_prev)
    def _():
        c_arrival(2).wait_recv()
        c_arrival(3).wait_recv()

    for t in range(2):
        q_local(t).wait()
    for r in range(4):
        for dc in range(2):
            for t in range(2):
                if r or dc:
                    q_copy(t, (4 - r) % 4, dc).wait_recv()

    nblk = jnp.where(has_prev, 4, 2)

    def lanes(b, j):
        return pl.ds(pl.multiple_of(b * BK + j * 128, 128), 128)

    def row_set(rel, _):
        mx[...] = jnp.full(mx.shape, MASKED, F32)

        def scores(b, _):
            keys = kvg[0, pl.ds(pl.multiple_of(b * BK, BK), BK), :]
            for h in range(NH):
                r = slice(h * SET, h * SET + SET)
                s = lax.dot_general(
                    qraw[rel, :, h * HEAD : h * HEAD + HEAD], keys, NT, preferred_element_type=F32
                )
                m = mx[r, :]
                for j in range(BK // 128):
                    sj = jnp.where(pk[0:1, lanes(b, j)] <= pq[rel], s[:, j * 128 : j * 128 + 128], MASKED)
                    m = jnp.maximum(m, sj)
                    s_buf[r, lanes(b, j)] = sj
                mx[r, :] = m
            return 0

        lax.fori_loop(0, nblk, scores, 0)
        for h in range(NH):
            r = slice(h * SET, h * SET + SET)
            mx[r, :] = jnp.broadcast_to(jnp.max(mx[r, :], axis=1, keepdims=True) * SCALE2, (SET, 128))
        ls[...] = jnp.zeros_like(ls)
        dd[...] = jnp.zeros_like(dd)

        def weights(b, _):
            vals = kvg[1, pl.ds(pl.multiple_of(b * BK, BK), BK), :]
            for h in range(NH):
                dp = lax.dot_general(
                    doraw[rel, :, h * HEAD : h * HEAD + HEAD], vals, NT, preferred_element_type=F32
                )
                for g0 in range(0, SET, VR):
                    g = slice(h * SET + g0, h * SET + g0 + VR)
                    m, l, d = mx[g, :], ls[g, :], dd[g, :]
                    for j in range(BK // 128):
                        e = jnp.exp2(s_buf[g, lanes(b, j)] * SCALE2 - m)
                        dpj = dp[g0 : g0 + VR, j * 128 : j * 128 + 128]
                        l = l + e
                        d = d + e * dpj
                        e_buf[g, lanes(b, j)] = e.astype(BF16)
                        dp_buf[g, lanes(b, j)] = dpj
                    ls[g, :] = l
                    dd[g, :] = d
            return 0

        lax.fori_loop(0, nblk, weights, 0)
        for h in range(NH):
            r = slice(h * SET, h * SET + SET)
            rinv = 1.0 / jnp.sum(ls[r, :], axis=1, keepdims=True)
            delta = jnp.sum(dd[r, :], axis=1, keepdims=True) * rinv
            ls[r, :] = jnp.broadcast_to(rinv, (SET, 128))
            dd[r, :] = jnp.broadcast_to(delta, (SET, 128))
            hc = slice(h * HEAD, h * HEAD + HEAD)
            qt[:, r] = (qraw[rel, :, hc].astype(F32) * rinv).astype(BF16).T
            dot[:, r] = (doraw[rel, :, hc].astype(F32) * rinv).astype(BF16).T
        dqa[...] = jnp.zeros_like(dqa)

        def grads(b, _):
            at = pl.ds(pl.multiple_of(b * BK, BK), BK)
            keys = kvg[0, at, :]
            dv = jnp.dot(dot[...], e_buf[:, at], preferred_element_type=F32)
            dk = None
            for h in range(NH):
                r = slice(h * SET, h * SET + SET)
                parts = []
                for g0 in range(0, SET, VR):
                    g = slice(h * SET + g0, h * SET + g0 + VR)
                    d = dd[g, :]
                    parts.append(
                        jnp.concatenate(
                            [
                                (e_buf[g, lanes(b, j)].astype(F32) * (dp_buf[g, lanes(b, j)] - d)).astype(BF16)
                                for j in range(BK // 128)
                            ],
                            axis=1,
                        )
                    )
                ds = jnp.concatenate(parts, axis=0)
                dqa[r, :] += jnp.dot(ds, keys, preferred_element_type=F32)
                part = jnp.dot(qt[:, r], ds, preferred_element_type=F32)
                dk = part if dk is None else dk + part
            for j in range(BK // 128):
                blk = b * (BK // 128) + j
                dva[blk] += dv[:, j * 128 : j * 128 + 128]
                dka[blk] += dk[:, j * 128 : j * 128 + 128]
            return 0

        lax.fori_loop(0, nblk, grads, 0)
        for h in range(NH):
            r = slice(h * SET, h * SET + SET)
            dqs[rel, :, h * HEAD : h * HEAD + HEAD] = (dqa[r, :] * (ls[r, :] * SCALE)).astype(BF16)
        return 0

    lax.fori_loop(0, 4, row_set, 0)

    mine = pl.ds(pl.multiple_of((y * 2 + c) * COLS, 128), COLS)

    def dq_copy(r, dc):
        cc = 1 - c if dc else c
        src = dqs.at[r, pl.ds(pl.multiple_of(cc * TOK, TOK), TOK)]
        return remote(
            src, gq_ref.at[:, mine], dq_ssem.at[r, dc], dq_rsem.at[(4 - r) % 4, dc], dev(o, yrel(r), xl, cc)
        )

    def dq_arrival(r, dc):
        cc = 1 - c if dc else c
        dst = gq_ref.at[:, pl.ds(pl.multiple_of((yrel(r) * 2 + cc) * COLS, 128), COLS)]
        return remote(dst, dst, dq_ssem.at[0, 1], dq_rsem.at[r, dc], core)

    for r in range(4):
        for dc in range(2):
            if r or dc:
                dq_copy(r, dc).start()
    dq_local = pltpu.make_async_copy(
        dqs.at[0, pl.ds(pl.multiple_of(c * TOK, TOK), TOK)], gq_ref.at[:, mine], l_sem.at[4]
    )
    dq_local.start()

    acc = (dka, dva)

    def rc_copy(seg):
        return remote(cx.at[seg], rx.at[seg], rc_ssem.at[seg], rc_rsem.at[seg], core)

    def rx_copy(n):
        if n == 0:
            return remote(xs.at[0], xr.at[0], rx_ssem.at[0], rx_rsem.at[0], dev(o, y, 1 - xl, c))
        return remote(xs.at[n], xr.at[1 + xl], rx_ssem.at[n], rx_rsem.at[1 + xl], dev(o_prev, y, n - 1, c))

    def rx_arrival(n):
        return remote(xr.at[n], xr.at[n], rx_ssem.at[0], rx_rsem.at[n], core)

    def ry_copy(d):
        yy = yrel(d)
        return remote(ys.at[yy], yr.at[y], ry_ssem.at[d - 1], ry_rsem.at[3 - d], dev(o, yy, xl, c))

    def ry_arrival(r):
        dst = yr.at[yrel(r)]
        return remote(dst, dst, ry_ssem.at[0], ry_rsem.at[r - 1], core)

    def send_core(seg):
        def step(yy, _):
            for t in range(2):
                cx[seg, t, yy] = acc[t][seg * 8 + (1 - c) * 4 + yy].astype(BF16)
            return 0

        lax.fori_loop(0, 4, step, 0)
        rc_copy(seg).start()

    def send_x(seg):
        rc_copy(seg).wait_recv()

        def step(yy, _):
            for t in range(2):
                xs[seg - 1, t, yy] = (acc[t][seg * 8 + c * 4 + yy] + rx[seg, t, yy].astype(F32)).astype(BF16)
            return 0

        lax.fori_loop(0, 4, step, 0)
        rx_copy(seg - 1).start()

    @pl.when(has_prev)
    def _():
        send_core(2)
        send_core(3)

    send_core(1)
    send_core(0)

    @pl.when(has_prev)
    def _():
        send_x(2)
        send_x(3)

    send_x(1)
    rc_copy(0).wait_recv()

    def own(yy, _):
        for t in range(2):
            blk = c * 4 + yy
            acc[t][blk] = acc[t][blk] + rx[0, t, yy].astype(F32)
        return 0

    lax.fori_loop(0, 4, own, 0)

    def take(n):
        rx_arrival(n).wait_recv()

        def step(yy, _):
            for t in range(2):
                blk = c * 4 + yy
                acc[t][blk] = acc[t][blk] + xr[n, t, yy].astype(F32)
            return 0

        lax.fori_loop(0, 4, step, 0)

    take(0)

    @pl.when(has_next)
    def _():
        take(1)
        take(2)

    def final(yy, _):
        blk = c * 4 + yy
        ys[yy, 0] = (acc[0][blk] * SCALE).astype(BF16)
        ys[yy, 1] = acc[1][blk].astype(BF16)
        return 0

    lax.fori_loop(0, 4, final, 0)
    for d in range(1, 4):
        ry_copy(d).start()
    outs = (gk_ref, gv_ref)
    at_me = pl.ds(pl.multiple_of(y * HEAD, HEAD), HEAD)
    for t in range(2):
        outs[t][:, at_me] = ys[y, t].T
    for r in range(1, 4):
        ry_arrival(r).wait_recv()
        at = pl.ds(pl.multiple_of(yrel(r) * HEAD, HEAD), HEAD)
        for t in range(2):
            outs[t][:, at] = yr[yrel(r), t].T

    dq_local.wait()
    for r in range(4):
        for dc in range(2):
            if r or dc:
                dq_arrival(r, dc).wait_recv()
                dq_copy(r, dc).wait_send()
                for t in range(2):
                    q_copy(t, r, dc).wait_send()
    for d in range(1, 4):
        ry_copy(d).wait_send()
        for t in range(2):
            kv_copy(t, d).wait_send()
    x_copy(0).wait_send()
    rx_copy(0).wait_send()
    for seg in range(2):
        c_copy(seg).wait_send()
        rc_copy(seg).wait_send()

    @pl.when(has_next)
    def _():
        x_copy(1).wait_send()
        x_copy(2).wait_send()

    @pl.when(has_prev)
    def _():
        for seg in (2, 3):
            c_copy(seg).wait_send()
            rc_copy(seg).wait_send()
            rx_copy(seg - 1).wait_send()


def on_device(queries, keys, values, output_gradient, span_order):
    vmem = pl.BlockSpec(memory_space=pltpu.VMEM)
    dma = pltpu.SemaphoreType.DMA
    return pl.pallas_call(
        kernel,
        out_shape=[
            jax.ShapeDtypeStruct(queries.shape, BF16),
            jax.ShapeDtypeStruct(keys.shape, BF16),
            jax.ShapeDtypeStruct(values.shape, BF16),
        ],
        in_specs=[vmem, vmem, vmem, vmem, pl.BlockSpec(memory_space=pltpu.SMEM)],
        out_specs=[vmem, vmem, vmem],
        scratch_shapes=[
            pltpu.VMEM((4, SET, COLS), BF16),
            pltpu.VMEM((4, SET, COLS), BF16),
            pltpu.VMEM((2, NKEY, HEAD), BF16),
            pltpu.VMEM((8, NKEY), F32),
            pltpu.VMEM((4, SET, 128), F32),
            pltpu.VMEM((HEAD, ROWS), BF16),
            pltpu.VMEM((HEAD, ROWS), BF16),
            pltpu.VMEM((ROWS, NKEY), F32),
            pltpu.VMEM((ROWS, NKEY), F32),
            pltpu.VMEM((ROWS, NKEY), BF16),
            pltpu.VMEM((ROWS, 128), F32),
            pltpu.VMEM((ROWS, 128), F32),
            pltpu.VMEM((ROWS, 128), F32),
            pltpu.VMEM((ROWS, HEAD), F32),
            pltpu.VMEM((32, HEAD, 128), F32),
            pltpu.VMEM((32, HEAD, 128), F32),
            pltpu.VMEM((4, SET, COLS), BF16),
            pltpu.VMEM((4, 2, 4, HEAD, 128), BF16),
            pltpu.VMEM((4, 2, 4, HEAD, 128), BF16),
            pltpu.VMEM((3, 2, 4, HEAD, 128), BF16),
            pltpu.VMEM((3, 2, 4, HEAD, 128), BF16),
            pltpu.VMEM((4, 2, HEAD, 128), BF16),
            pltpu.VMEM((4, 2, HEAD, 128), BF16),
            dma((2, 4, 2)), dma((2, 4, 2)),
            dma((2, 3)), dma((2, 3)),
            dma((3,)), dma((3,)),
            dma((4,)), dma((4,)),
            dma((5,)),
            dma((4, 2)), dma((4, 2)),
            dma((4,)), dma((4,)),
            dma((3,)), dma((3,)),
            dma((3,)), dma((3,)),
        ],
        compiler_params=pltpu.CompilerParams(
            collective_id=0, has_side_effects=True, vmem_limit_bytes=60 * 2**20
        ),
        name="attention_backward",
    )(queries, keys, values, output_gradient, span_order)


def solution(mesh):
    rows = P(("outer", "inner"), None)
    return jax.shard_map(
        on_device,
        mesh=mesh,
        in_specs=(rows, rows, rows, rows, P()),
        out_specs=(rows, rows, rows),
        check_vma=False,
    )
```

time: 666 us -> 115 us (0.17); the launches traced: 657 us -> 114 us
  waiting for transfers between devices: 249 us -> 0 us
  matrix products: 192 us -> 0 us
  local copies, waits for them, and re-layouts: 140 us -> 3.71 us
  Pallas kernels: 0 us -> 109 us
  other arithmetic: 45.6 us -> 0 us
  starting transfers between devices: 15.1 us -> 0 us
  between operations: 14.4 us -> 0.65 us
    dot_general x64 -> x0, matrix products: 192 us -> none  [the longest x24 71.9 us: block_scores(): jnp.einsum('hoxz,qhz->hoxq', query_transposed, block_of_keys, preferred_e...]
    reduce_scatter x4 -> x0, waiting for transfers between devices: 180 us -> none  [the longest x1 64.1 us: on_device(): lax.psum_scatter(dk_terms[group_len:].astype(jnp.bfloat16), 'inner', scat...]
    pallas_call x0 -> x1, Pallas kernels: none -> 109 us  [on_device(): pl.pallas_call(kernel, out_shape=[jax.ShapeDtypeStruct(queries.shape, BF1...]
    all_gather x4 -> x0, waiting for transfers between devices: 55.2 us -> none  [the longest x1 36.5 us: on_device(): lax.all_gather(keys, 'inner', axis=0, tiled=True)]
    dynamic_update_slice x32 -> x0, local copies, waits for them, and re-layouts: 48.3 us -> none  [the longest x16 31.5 us: value_step(): lax.dynamic_update_slice_in_dim(dv_terms, dv_block, block_idx * block_len...]
    dynamic_slice x72 -> x0, local copies, waits for them, and re-layouts: 39 us -> none  [the longest x16 26.7 us: block_scores(): lax.dynamic_slice_in_dim(stacked_values, start, block_len, 0)]
    reduce_sum x11 -> x0, other arithmetic: 37.1 us -> none  [the longest x8 34.5 us: stats_step(): jnp.sum(jnp.where(visible, jnp.exp(scores - new_max[..., None]), 0.0), ax...]
    while x42 -> x0, local copies, waits for them, and re-layouts: 15.8 us -> none
  transfers between devices with their start and end apart: 12 -> 0, of which waited for: 7 -> 0; matrix products, arithmetic and copies ran while one was open for 33% -> 0% of each run, Pallas kernels for 0% -> 0%
where the time goes in v1:
time: 115 us; the launch traced here: 114 us
  Pallas kernels  109 us (95%)
  local copies, waits for them, and re-layouts  3.71 us (3%)
    pallas_call x1, Pallas kernels, on_device(): pl.pallas_call(kernel, out_shape=[jax.ShapeDtypeStruct(queries.shape, BF1...  109 us
    unnamed x7, local copies, waits for them, and re-layouts  3.71 us

profile of v1, /device:TPU:34, one launch (start us, length us, event | category | flops | bytes accessed | tf_op | source)
XLA Modules:
  0.0 113.8 jit_solution(16424870667905955346)
XLA Ops:
  0.6 109.4 %attention_backward.1 = (bf16[128,3072]{1,0:T(8,128)(2,1)}, bf16[128,512]{1,0:T(8,128)(2,1)}, bf16[128,512]{1,0:T(8,128)(2,1)}) custom-call(bf16[128,3072]{1,0:T(8,128)(2,1)} %q_ref.1, bf16[128,512]{1,0:T(8,128)(2,1)} %k_ref.1, bf16[128,512]{1,0:T(8,128)(2,1)} %v_ref.1, bf16[128,3072]{1,0:T(8,128)(2,1)} %do_ref.1, s32[32]{0:T(128)} %span_ref.1), custom_call_target="tpu_custom_call" | custom-call | tf_op jit(solution)/shard_map/attention_backward/pallas_call | solution.py:437
  110.0 0.0 copy-start.1
  110.1 2.1 %copy.11 = bf16[128,3072]{1,0:T(8,128)(2,1)} copy(bf16[128,3072]{1,0:T(8,128)(2,1)} %get-tuple-element.6) | data formatting | bytes 1572864
  112.2 0.0 copy-done.1
  112.2 0.0 copy-start
  112.2 0.7 copy.12
  112.8 0.3 copy-done
  113.1 0.7 copy.13
Async XLA Ops:
  110.0 2.1 %copy-start.1 = (bf16[128,512]{1,0:T(8,128)(2,1)S(1)}, bf16[128,512]{1,0:T(8,128)(2,1)}, u32[]{:S(2)}) copy-start(bf16[128,512]{1,0:T(8,128)(2,1)} %get-tuple-element.7) | copy-start | bytes 393220
  112.2 1.0 copy-start

commit v2 on v1

v2 whole, which is shorter than its diff:
```python
import jax
import jax.numpy as jnp
from jax import lax
from jax.experimental import pallas as pl
from jax.experimental.pallas import tpu as pltpu
from jax.sharding import PartitionSpec as P

MESH = pl.DeviceIdType.MESH
F32 = jnp.float32
BF16 = jnp.bfloat16
SCALE = 128**-0.5
SCALE2 = SCALE * 1.4426950408889634
MASKED = -1.0e30
NT = (((1,), (1,)), ((), ()))

HEAD = 128
TOK = 128
NH = 3
SET = 2 * TOK
ROWS = NH * SET
COLS = NH * HEAD
SEG = 8 * TOK
NKEY = 4 * SEG
VR = 16


def kernel(
    q_ref, k_ref, v_ref, do_ref, span_ref,
    gq_ref, gk_ref, gv_ref,
    qraw, doraw, kvg, pk, pq, qt, dot, s_buf, dp_buf, e_buf, mx, ls, dd, dqa, dka, dva, dqs,
    cx, rx, xs, xr, ys, yr,
    q_ssem, q_rsem, y_ssem, y_rsem, x_ssem, x_rsem, c_ssem, c_rsem, l_sem,
    dq_ssem, dq_rsem, rc_ssem, rc_rsem, rx_ssem, rx_rsem, ry_ssem, ry_rsem,
):
    o = lax.axis_index("outer")
    i = lax.axis_index("inner")
    y, xl, c = i // 4, (i // 2) % 2, i % 2
    has_prev = o > 0
    has_next = o < 7

    def dev(oo, yy, xx, cc):
        return (oo, yy * 4 + xx * 2 + cc)

    def yrel(d):
        return lax.rem(y + d, 4)

    def remote(src, dst, ssem, rsem, device):
        return pltpu.make_async_remote_copy(
            src_ref=src, dst_ref=dst, send_sem=ssem, recv_sem=rsem, device_id=device, device_id_type=MESH
        )

    o_next, o_prev = lax.rem(o + 1, 8), lax.rem(o + 7, 8)
    core = dev(o, y, xl, 1 - c)

    barrier = pltpu.get_barrier_semaphore()
    peers = [dev(o, yrel(d), xl, cc) for d in range(1, 4) for cc in range(2)]
    peers += [core, dev(o, y, 1 - xl, c)]
    peers += [dev(oo, y, xx, c) for oo in (o_next, o_prev) for xx in range(2)]
    for p in peers:
        pl.semaphore_signal(barrier, inc=1, device_id=p, device_id_type=MESH)
    pl.semaphore_wait(barrier, len(peers))

    def rows(seg, cc, yy=0, n=4):
        return pl.ds(pl.multiple_of(seg * SEG + cc * 4 * TOK + yy * TOK, TOK), n * TOK)

    def kv_copy(t, d):
        yy = yrel(d)
        src = (k_ref, v_ref)[t].at[:, pl.ds(pl.multiple_of(yy * HEAD, HEAD), HEAD)]
        return remote(src, kvg.at[t, rows(0, c, y, 1)], y_ssem.at[t, d - 1], y_rsem.at[t, 3 - d], dev(o, yy, xl, c))

    def kv_local(t):
        src = (k_ref, v_ref)[t].at[:, pl.ds(pl.multiple_of(y * HEAD, HEAD), HEAD)]
        return pltpu.make_async_copy(src, kvg.at[t, rows(0, c, y, 1)], l_sem.at[t])

    def q_copy(t, d, dc):
        yy, cc = yrel(d), (1 - c if dc else c)
        src = (q_ref, do_ref)[t].at[:, pl.ds(pl.multiple_of((yy * 2 + cc) * COLS, 128), COLS)]
        r = lax.rem(4 - d, 4)
        dst = (qraw, doraw)[t].at[r, pl.ds(pl.multiple_of(c * TOK, TOK), TOK)]
        return remote(src, dst, q_ssem.at[t, d, dc], q_rsem.at[t, r, dc], dev(o, yy, xl, cc))

    def q_local(t):
        src = (q_ref, do_ref)[t].at[:, pl.ds(pl.multiple_of((y * 2 + c) * COLS, 128), COLS)]
        dst = (qraw, doraw)[t].at[0, pl.ds(pl.multiple_of(c * TOK, TOK), TOK)]
        return pltpu.make_async_copy(src, dst, l_sem.at[2 + t])

    def x_copy(n, d):
        yy = yrel(d)
        src = kvg.at[:, rows(0, c, yy, 1)]
        if n == 0:
            dst, device, slot = kvg.at[:, rows(1, c, yy, 1)], dev(o, y, 1 - xl, c), 0
        else:
            dst, device, slot = kvg.at[:, rows(2 + xl, c, yy, 1)], dev(o_next, y, n - 1, c), 1 + xl
        return remote(src, dst, x_ssem.at[n, d], x_rsem.at[slot, d], device)

    def x_arrival(n, d):
        dst = kvg.at[:, rows(1 + n, c, yrel(d), 1)]
        return remote(dst, dst, x_ssem.at[0, 0], x_rsem.at[n, d], core)

    def c_copy(seg):
        blk = kvg.at[:, rows(seg, c)]
        return remote(blk, blk, c_ssem.at[seg], c_rsem.at[seg], core)

    def c_arrival(seg):
        blk = kvg.at[:, rows(seg, 1 - c)]
        return remote(blk, blk, c_ssem.at[seg], c_rsem.at[seg], core)

    for t in range(2):
        kv_local(t).start()
        for d in (1, 3, 2):
            kv_copy(t, d).start()
    for t in range(2):
        q_local(t).start()
        q_copy(t, 0, 1).start()

    def send_column(d):
        x_copy(0, d).start()

        @pl.when(has_next)
        def _():
            x_copy(1, d).start()
            x_copy(2, d).start()

    for t in range(2):
        kv_local(t).wait()
    send_column(0)
    for d in (3, 1, 2):
        for dc in range(2):
            for t in range(2):
                q_copy(t, d, dc).start()

    def pk_row(blk, value):
        pk[blk] = value

    lane = lax.broadcasted_iota(jnp.int32, (8, TOK), 1)
    for xx in range(2):
        for cc in range(2):
            for yy in range(4):
                first = 2 * (yy * 4 + xx * 2 + cc)
                span = jnp.where(lane < 64, span_ref[first], span_ref[first + 1])
                blk = jnp.where(xl == xx, 0, 8) + cc * 4 + yy
                pk_row(blk, (span * 64 + lax.rem(lane, 64)).astype(F32))
    for blk in range(16, 32):
        pk_row(blk, jnp.full((8, TOK), -1.0, F32))
    sub = lax.broadcasted_iota(jnp.int32, (64, 128), 0)
    for rel in range(4):
        for cc in range(2):
            for hb in range(2):
                span = span_ref[2 * (yrel(rel) * 4 + xl * 2 + cc) + hb]
                at = (cc * 2 + hb) * 64
                pq[rel, at : at + 64, :] = (span * 64 + sub).astype(F32)

    dka[...] = jnp.zeros_like(dka)
    dva[...] = jnp.zeros_like(dva)

    for d in (3, 1, 2):
        for t in range(2):
            kv_copy(t, 4 - d).wait_recv()
        send_column(d)
    c_copy(0).start()
    c_arrival(0).wait_recv()
    for d in range(4):
        x_arrival(0, d).wait_recv()
    c_copy(1).start()
    for t in range(2):
        q_local(t).wait()
        q_copy(t, 0, 1).wait_recv()
    c_arrival(1).wait_recv()

    def take_previous():
        for n in (1, 2):
            for d in range(4):
                x_arrival(n, d).wait_recv()
            c_copy(1 + n).start()
        for n in (1, 2):
            c_arrival(1 + n).wait_recv()

    mine = pl.ds(pl.multiple_of((y * 2 + c) * COLS, 128), COLS)

    def dq_copy(r, dc):
        cc = 1 - c if dc else c
        src = dqs.at[r, pl.ds(pl.multiple_of(cc * TOK, TOK), TOK)]
        return remote(
            src,
            gq_ref.at[:, mine],
            dq_ssem.at[r, dc],
            dq_rsem.at[lax.rem(4 - r, 4), dc],
            dev(o, yrel(r), xl, cc),
        )

    def dq_arrival(r, dc):
        cc = 1 - c if dc else c
        dst = gq_ref.at[:, pl.ds(pl.multiple_of((yrel(r) * 2 + cc) * COLS, 128), COLS)]
        return remote(dst, dst, dq_ssem.at[0, 1], dq_rsem.at[r, dc], core)

    dq_local = pltpu.make_async_copy(
        dqs.at[0, pl.ds(pl.multiple_of(c * TOK, TOK), TOK)], gq_ref.at[:, mine], l_sem.at[4]
    )

    acc = (dka, dva)

    def rc_copy(seg):
        return remote(cx.at[seg], rx.at[seg], rc_ssem.at[seg], rc_rsem.at[seg], core)

    def rx_copy(n):
        if n == 0:
            return remote(xs.at[0], xr.at[0], rx_ssem.at[0], rx_rsem.at[0], dev(o, y, 1 - xl, c))
        return remote(xs.at[n], xr.at[1 + xl], rx_ssem.at[n], rx_rsem.at[1 + xl], dev(o_prev, y, n - 1, c))

    def rx_arrival(n):
        return remote(xr.at[n], xr.at[n], rx_ssem.at[0], rx_rsem.at[n], core)

    def ry_copy(d):
        yy = yrel(d)
        return remote(ys.at[yy], yr.at[y], ry_ssem.at[d - 1], ry_rsem.at[3 - d], dev(o, yy, xl, c))

    def ry_arrival(r):
        dst = yr.at[yrel(r)]
        return remote(dst, dst, ry_ssem.at[0], ry_rsem.at[r - 1], core)

    def send_core(seg):
        def step(yy, _):
            for t in range(2):
                cx[seg, t, yy] = acc[t][seg * 8 + (1 - c) * 4 + yy].astype(BF16)
            return 0

        lax.fori_loop(0, 4, step, 0)
        rc_copy(seg).start()

    def send_x(seg):
        rc_copy(seg).wait_recv()

        def step(yy, _):
            for t in range(2):
                xs[seg - 1, t, yy] = (acc[t][seg * 8 + c * 4 + yy] + rx[seg, t, yy].astype(F32)).astype(BF16)
            return 0

        lax.fori_loop(0, 4, step, 0)
        rx_copy(seg - 1).start()

    npair = jnp.where(has_prev, 2, 1)
    nl = SEG // 128

    def row_set(rel, _):
        @pl.when(rel > 0)
        def _():
            for dc in range(2):
                for t in range(2):
                    q_copy(t, 4 - rel, dc).wait_recv()

        mx[...] = jnp.full(mx.shape, MASKED, F32)

        def scores(pair, _):
            @pl.when((rel == 0) & (pair == 1))
            def _():
                take_previous()

            for half in range(2):
                b = pair * 2 + half
                keys = kvg[0, pl.ds(pl.multiple_of(b * SEG, SEG), SEG), :]
                for h in range(NH):
                    r = slice(h * SET, h * SET + SET)
                    s = lax.dot_general(
                        qraw[rel, :, h * HEAD : h * HEAD + HEAD], keys, NT, preferred_element_type=F32
                    )
                    m = mx[r, :]
                    for j in range(nl):
                        at = slice(j * 128, j * 128 + 128)
                        sj = jnp.where(pk[b * nl + j, 0:1, :] <= pq[rel], s[:, at], MASKED)
                        m = jnp.maximum(m, sj)
                        s_buf[b, r, at] = sj
                    mx[r, :] = m
            return 0

        lax.fori_loop(0, npair, scores, 0)
        for h in range(NH):
            r = slice(h * SET, h * SET + SET)
            mx[r, :] = jnp.broadcast_to(jnp.max(mx[r, :], axis=1, keepdims=True) * SCALE2, (SET, 128))
        ls[...] = jnp.zeros_like(ls)
        dd[...] = jnp.zeros_like(dd)

        def weights(pair, _):
            for half in range(2):
                b = pair * 2 + half
                vals = kvg[1, pl.ds(pl.multiple_of(b * SEG, SEG), SEG), :]
                for h in range(NH):
                    dp = lax.dot_general(
                        doraw[rel, :, h * HEAD : h * HEAD + HEAD], vals, NT, preferred_element_type=F32
                    )
                    for g0 in range(0, SET, VR):
                        g = slice(h * SET + g0, h * SET + g0 + VR)
                        m, l, d = mx[g, :], ls[g, :], dd[g, :]
                        for j in range(nl):
                            at = slice(j * 128, j * 128 + 128)
                            e = jnp.exp2(s_buf[b, g, at] * SCALE2 - m)
                            dpj = dp[g0 : g0 + VR, at]
                            l = l + e
                            d = d + e * dpj
                            e_buf[b, g, at] = e.astype(BF16)
                            dp_buf[b, g, at] = dpj
                        ls[g, :] = l
                        dd[g, :] = d
            return 0

        lax.fori_loop(0, npair, weights, 0)
        for h in range(NH):
            r = slice(h * SET, h * SET + SET)
            rinv = 1.0 / jnp.sum(ls[r, :], axis=1, keepdims=True)
            delta = jnp.sum(dd[r, :], axis=1, keepdims=True) * rinv
            ls[r, :] = jnp.broadcast_to(rinv, (SET, 128))
            dd[r, :] = jnp.broadcast_to(delta, (SET, 128))
            hc = slice(h * HEAD, h * HEAD + HEAD)
            qt[:, r] = (qraw[rel, :, hc].astype(F32) * rinv).astype(BF16).T
            dot[:, r] = (doraw[rel, :, hc].astype(F32) * rinv).astype(BF16).T
        dqa[...] = jnp.zeros_like(dqa)

        def grads(step, _):
            pair = npair - 1 - step
            for half in range(2):
                b = pair * 2 + half
                keys = kvg[0, pl.ds(pl.multiple_of(b * SEG, SEG), SEG), :]
                dv = jnp.dot(dot[...], e_buf[b], preferred_element_type=F32)
                dk = None
                for h in range(NH):
                    r = slice(h * SET, h * SET + SET)
                    parts = []
                    for g0 in range(0, SET, VR):
                        g = slice(h * SET + g0, h * SET + g0 + VR)
                        d = dd[g, :]
                        part = []
                        for j in range(nl):
                            at = slice(j * 128, j * 128 + 128)
                            part.append((e_buf[b, g, at].astype(F32) * (dp_buf[b, g, at] - d)).astype(BF16))
                        parts.append(jnp.concatenate(part, axis=1))
                    ds = jnp.concatenate(parts, axis=0)
                    dqa[r, :] += jnp.dot(ds, keys, preferred_element_type=F32)
                    part = jnp.dot(qt[:, r], ds, preferred_element_type=F32)
                    dk = part if dk is None else dk + part
                for j in range(nl):
                    blk = b * nl + j
                    dva[blk] += dv[:, j * 128 : j * 128 + 128]
                    dka[blk] += dk[:, j * 128 : j * 128 + 128]

            @pl.when((rel == 3) & (pair == 1))
            def _():
                send_core(2)
                send_core(3)

            return 0

        lax.fori_loop(0, npair, grads, 0)
        for h in range(NH):
            r = slice(h * SET, h * SET + SET)
            dqs[rel, :, h * HEAD : h * HEAD + HEAD] = (dqa[r, :] * (ls[r, :] * SCALE)).astype(BF16)

        @pl.when(rel > 0)
        def _():
            dq_copy(rel, 0).start()

        @pl.when(rel == 0)
        def _():
            dq_local.start()

        dq_copy(rel, 1).start()
        return 0

    lax.fori_loop(0, 4, row_set, 0)

    send_core(1)
    send_core(0)

    @pl.when(has_prev)
    def _():
        send_x(2)
        send_x(3)

    send_x(1)
    rc_copy(0).wait_recv()

    def own(yy, _):
        for t in range(2):
            blk = c * 4 + yy
            acc[t][blk] = acc[t][blk] + rx[0, t, yy].astype(F32)
        return 0

    lax.fori_loop(0, 4, own, 0)

    def take(n):
        rx_arrival(n).wait_recv()

        def step(yy, _):
            for t in range(2):
                blk = c * 4 + yy
                acc[t][blk] = acc[t][blk] + xr[n, t, yy].astype(F32)
            return 0

        lax.fori_loop(0, 4, step, 0)

    take(0)

    @pl.when(has_next)
    def _():
        take(1)
        take(2)

    def final(yy, _):
        blk = c * 4 + yy
        ys[yy, 0] = (acc[0][blk] * SCALE).astype(BF16)
        ys[yy, 1] = acc[1][blk].astype(BF16)
        return 0

    lax.fori_loop(0, 4, final, 0)
    for d in range(1, 4):
        ry_copy(d).start()
    outs = (gk_ref, gv_ref)
    at_me = pl.ds(pl.multiple_of(y * HEAD, HEAD), HEAD)
    for t in range(2):
        outs[t][:, at_me] = ys[y, t].T
    for r in range(1, 4):
        ry_arrival(r).wait_recv()
        at = pl.ds(pl.multiple_of(yrel(r) * HEAD, HEAD), HEAD)
        for t in range(2):
            outs[t][:, at] = yr[yrel(r), t].T

    dq_local.wait()
    for r in range(4):
        for dc in range(2):
            if r or dc:
                dq_arrival(r, dc).wait_recv()
                dq_copy(r, dc).wait_send()
                for t in range(2):
                    q_copy(t, r, dc).wait_send()
    for d in range(1, 4):
        ry_copy(d).wait_send()
        for t in range(2):
            kv_copy(t, d).wait_send()
    for d in range(4):
        x_copy(0, d).wait_send()
    rx_copy(0).wait_send()
    for seg in range(2):
        c_copy(seg).wait_send()
        rc_copy(seg).wait_send()

    @pl.when(has_next)
    def _():
        for d in range(4):
            x_copy(1, d).wait_send()
            x_copy(2, d).wait_send()

    @pl.when(has_prev)
    def _():
        for seg in (2, 3):
            c_copy(seg).wait_send()
            rc_copy(seg).wait_send()
            rx_copy(seg - 1).wait_send()


def on_device(queries, keys, values, output_gradient, span_order):
    vmem = pl.BlockSpec(memory_space=pltpu.VMEM)
    dma = pltpu.SemaphoreType.DMA
    return pl.pallas_call(
        kernel,
        out_shape=[
            jax.ShapeDtypeStruct(queries.shape, BF16),
            jax.ShapeDtypeStruct(keys.shape, BF16),
            jax.ShapeDtypeStruct(values.shape, BF16),
        ],
        in_specs=[vmem, vmem, vmem, vmem, pl.BlockSpec(memory_space=pltpu.SMEM)],
        out_specs=[vmem, vmem, vmem],
        scratch_shapes=[
            pltpu.VMEM((4, SET, COLS), BF16),
            pltpu.VMEM((4, SET, COLS), BF16),
            pltpu.VMEM((2, NKEY, HEAD), BF16),
            pltpu.VMEM((32, 8, TOK), F32),
            pltpu.VMEM((4, SET, 128), F32),
            pltpu.VMEM((HEAD, ROWS), BF16),
            pltpu.VMEM((HEAD, ROWS), BF16),
            pltpu.VMEM((4, ROWS, SEG), F32),
            pltpu.VMEM((4, ROWS, SEG), F32),
            pltpu.VMEM((4, ROWS, SEG), BF16),
            pltpu.VMEM((ROWS, 128), F32),
            pltpu.VMEM((ROWS, 128), F32),
            pltpu.VMEM((ROWS, 128), F32),
            pltpu.VMEM((ROWS, HEAD), F32),
            pltpu.VMEM((32, HEAD, 128), F32),
            pltpu.VMEM((32, HEAD, 128), F32),
            pltpu.VMEM((4, SET, COLS), BF16),
            pltpu.VMEM((4, 2, 4, HEAD, 128), BF16),
            pltpu.VMEM((4, 2, 4, HEAD, 128), BF16),
            pltpu.VMEM((3, 2, 4, HEAD, 128), BF16),
            pltpu.VMEM((3, 2, 4, HEAD, 128), BF16),
            pltpu.VMEM((4, 2, HEAD, 128), BF16),
            pltpu.VMEM((4, 2, HEAD, 128), BF16),
            dma((2, 4, 2)), dma((2, 4, 2)),
            dma((2, 3)), dma((2, 3)),
            dma((3, 4)), dma((3, 4)),
            dma((4,)), dma((4,)),
            dma((5,)),
            dma((4, 2)), dma((4, 2)),
            dma((4,)), dma((4,)),
            dma((3,)), dma((3,)),
            dma((3,)), dma((3,)),
        ],
        compiler_params=pltpu.CompilerParams(
            collective_id=0, has_side_effects=True, vmem_limit_bytes=60 * 2**20
        ),
        name="attention_backward",
    )(queries, keys, values, output_gradient, span_order)


def solution(mesh):
    rows = P(("outer", "inner"), None)
    return jax.shard_map(
        on_device,
        mesh=mesh,
        in_specs=(rows, rows, rows, rows, P()),
        out_specs=(rows, rows, rows),
        check_vma=False,
    )
```

time: 115 us -> 89.2 us (0.78)
  the two profiles are of different devices: /device:TPU:34 before, /device:TPU:1 now
where the time goes in v2:
time: 89.2 us; the launch traced here: 89 us
  Pallas kernels  84.7 us (95%)
  local copies, waits for them, and re-layouts  3.71 us (4%)
    pallas_call x1, Pallas kernels, on_device(): pl.pallas_call(kernel, out_shape=[jax.ShapeDtypeStruct(queries.shape, BF1...  84.7 us
    unnamed x7, local copies, waits for them, and re-layouts  3.71 us

profile of v2, /device:TPU:1, one launch (start us, length us, event | category | flops | bytes accessed | tf_op | source)
XLA Modules:
  0.0 89.0 jit_solution(11545801593688625229)
XLA Ops:
  0.6 84.7 %attention_backward.1 = (bf16[128,3072]{1,0:T(8,128)(2,1)}, bf16[128,512]{1,0:T(8,128)(2,1)}, bf16[128,512]{1,0:T(8,128)(2,1)}) custom-call(bf16[128,3072]{1,0:T(8,128)(2,1)} %q_ref.1, bf16[128,512]{1,0:T(8,128)(2,1)} %k_ref.1, bf16[128,512]{1,0:T(8,128)(2,1)} %v_ref.1, bf16[128,3072]{1,0:T(8,128)(2,1)} %do_ref.1, s32[32]{0:T(128)} %span_ref.1), custom_call_target="tpu_custom_call" | custom-call | tf_op jit(solution)/shard_map/attention_backward/pallas_call | solution.py:461
  85.3 0.0 copy-start.1
  85.3 2.1 %copy.11 = bf16[128,3072]{1,0:T(8,128)(2,1)} copy(bf16[128,3072]{1,0:T(8,128)(2,1)} %get-tuple-element.6) | data formatting | bytes 1572864
  87.4 0.0 copy-done.1
  87.4 0.0 copy-start
  87.4 0.7 copy.12
  88.1 0.3 copy-done
  88.4 0.7 copy.13
Async XLA Ops:
  85.3 2.1 %copy-start.1 = (bf16[128,512]{1,0:T(8,128)(2,1)S(1)}, bf16[128,512]{1,0:T(8,128)(2,1)}, u32[]{:S(2)}) copy-start(bf16[128,512]{1,0:T(8,128)(2,1)} %get-tuple-element.7) | copy-start | bytes 393220
  87.4 1.0 %copy-start = (bf16[128,512]{1,0:T(8,128)(2,1)S(1)}, bf16[128,512]{1,0:T(8,128)(2,1)}, u32[]{:S(2)}) copy-start(bf16[128,512]{1,0:T(8,128)(2,1)} %get-tuple-element.8) | copy-start | bytes 393220

commit v3 on v2

--- a/solution.py
+++ b/solution.py
@@ -27,7 +27,7 @@
 def kernel(
     q_ref, k_ref, v_ref, do_ref, span_ref,
     gq_ref, gk_ref, gv_ref,
-    qraw, doraw, kvg, pk, pq, qt, dot, s_buf, dp_buf, e_buf, mx, ls, dd, dqa, dka, dva, dqs,
+    qraw, doraw, kvg, pk, pq, qt, dot, s_buf, e_buf, mx, wgt, st_l, st_d, dqp, dka, dva, dqs,
     cx, rx, xs, xr, ys, yr,
     q_ssem, q_rsem, y_ssem, y_rsem, x_ssem, x_rsem, c_ssem, c_rsem, l_sem,
     dq_ssem, dq_rsem, rc_ssem, rc_rsem, rx_ssem, rx_rsem, ry_ssem, ry_rsem,
@@ -113,9 +113,7 @@
         q_local(t).start()
         q_copy(t, 0, 1).start()
 
-    def send_column(d):
-        x_copy(0, d).start()
-
+    def send_next(d):
         @pl.when(has_next)
         def _():
             x_copy(1, d).start()
@@ -123,12 +121,8 @@
 
     for t in range(2):
         kv_local(t).wait()
-    send_column(0)
-    for d in (3, 1, 2):
-        for dc in range(2):
-            for t in range(2):
-                q_copy(t, d, dc).start()
-
+    x_copy(0, 0).start()
+    send_next(0)
     def pk_row(blk, value):
         pk[blk] = value
 
@@ -156,7 +150,13 @@
     for d in (3, 1, 2):
         for t in range(2):
             kv_copy(t, 4 - d).wait_recv()
-        send_column(d)
+        x_copy(0, d).start()
+    for d in (3, 1):
+        for dc in range(2):
+            for t in range(2):
+                q_copy(t, d, dc).start()
+    for d in (3, 1, 2):
+        send_next(d)
     c_copy(0).start()
     c_arrival(0).wait_recv()
     for d in range(4):
@@ -238,10 +238,52 @@
         lax.fori_loop(0, 4, step, 0)
         rx_copy(seg - 1).start()
 
-    npair = jnp.where(has_prev, 2, 1)
     nl = SEG // 128
-
-    def row_set(rel, _):
+    hrows = [slice(h * SET, h * SET + SET) for h in range(NH)]
+    hcols = [slice(h * HEAD, h * HEAD + HEAD) for h in range(NH)]
+
+    def lanes(j):
+        return slice(j * 128, j * 128 + 128)
+
+    def keys_of(t, seg):
+        return kvg[t, seg * SEG : seg * SEG + SEG, :]
+
+    def scores(rel, first, masked):
+        for half in range(2):
+            keys = keys_of(0, first + half)
+            for h in range(NH):
+                r = hrows[h]
+                s = lax.dot_general(qraw[rel, :, hcols[h]], keys, NT, preferred_element_type=F32)
+                m = mx[r, :]
+                for j in range(nl):
+                    sj = s[:, lanes(j)] * SCALE2
+                    if masked:
+                        sj = jnp.where(pk[(first + half) * nl + j, 0:1, :] <= pq[rel], sj, MASKED)
+                    m = jnp.maximum(m, sj)
+                    s_buf[half, r, lanes(j)] = sj
+                mx[r, :] = m
+
+    def weights(rel, first):
+        for half in range(2):
+            vals = keys_of(1, first + half)
+            for h in range(NH):
+                dp = lax.dot_general(doraw[rel, :, hcols[h]], vals, NT, preferred_element_type=F32)
+                for g0 in range(0, SET, VR):
+                    g = slice(h * SET + g0, h * SET + g0 + VR)
+                    m, l, d = mx[g, :], st_l[rel, g, :], st_d[rel, g, :]
+                    for j in range(nl):
+                        e = jnp.exp2(s_buf[half, g, lanes(j)] - m)
+                        dpj = dp[g0 : g0 + VR, lanes(j)]
+                        l = l + e
+                        d = d + e * dpj
+                        e_buf[first + half, rel, g, lanes(j)] = e.astype(BF16)
+                    st_l[rel, g, :] = l
+                    st_d[rel, g, :] = d
+
+    def scaled_t(x, w):
+        return (x.astype(F32) * w).astype(BF16).T
+
+    def own_keys(rel):
         @pl.when(rel > 0)
         def _():
             for dc in range(2):
@@ -249,132 +291,137 @@
                     q_copy(t, 4 - rel, dc).wait_recv()
 
         mx[...] = jnp.full(mx.shape, MASKED, F32)
-
-        def scores(pair, _):
-            @pl.when((rel == 0) & (pair == 1))
+        st_l[rel] = jnp.zeros((ROWS, 128), F32)
+        st_d[rel] = jnp.zeros((ROWS, 128), F32)
+        dqp[rel] = jnp.zeros((ROWS, HEAD), F32)
+        scores(rel, 0, True)
+        for r in hrows:
+            m = jnp.broadcast_to(jnp.max(mx[r, :], axis=1, keepdims=True), (SET, 128))
+            mx[r, :] = m
+            wgt[0, rel, r, :] = m
+        weights(rel, 0)
+
+    def previous_keys(rel):
+        @pl.when(has_prev)
+        def _():
+            mx[...] = jnp.full(mx.shape, MASKED, F32)
+            scores(rel, 2, False)
+            for r in hrows:
+                top = jnp.max(mx[r, :], axis=1, keepdims=True)
+                before = wgt[0, rel, r, :]
+                m = jnp.maximum(before, top)
+                shrink = jnp.exp2(before - m)
+                mx[r, :] = m
+                wgt[0, rel, r, :] = shrink
+                st_l[rel, r, :] = st_l[rel, r, :] * shrink
+                st_d[rel, r, :] = st_d[rel, r, :] * shrink
+            weights(rel, 2)
+
+        @pl.when(jnp.logical_not(has_prev))
+        def _():
+            wgt[0, rel] = jnp.ones((ROWS, 128), F32)
+
+        for h in range(NH):
+            r = hrows[h]
+            rinv = 1.0 / jnp.sum(st_l[rel, r, :], axis=1, keepdims=True)
+            delta = jnp.sum(st_d[rel, r, :], axis=1, keepdims=True) * rinv
+            st_d[rel, r, :] = jnp.broadcast_to(delta, (SET, 128))
+            factors = (wgt[0, rel, r, :] * rinv, jnp.broadcast_to(rinv, (SET, 128)))
+            for g in range(2):
+                wgt[g, rel, r, :] = factors[g]
+                qt[g, rel, :, r] = scaled_t(qraw[rel, :, hcols[h]], factors[g])
+                dot[g, rel, :, r] = scaled_t(doraw[rel, :, hcols[h]], factors[g])
+
+    def forward(step, _):
+        t = jnp.where(step >= 3, step - 3, step)
+        rel = jnp.where(step >= 6, 2, jnp.where(t == 2, 3, t))
+        own = (step < 3) | (step == 6)
+
+        @pl.when(step == 1)
+        def _():
+            for dc in range(2):
+                for t in range(2):
+                    q_copy(t, 2, dc).start()
+
+        @pl.when((step == 3) & has_prev)
+        def _():
+            take_previous()
+
+        @pl.when(own)
+        def _():
+            own_keys(rel)
+
+        @pl.when(jnp.logical_not(own))
+        def _():
+            previous_keys(rel)
+
+        return 0
+
+    lax.fori_loop(0, 8, forward, 0)
+
+    def gradients(it, _):
+        order = it // 4
+        seg = jnp.where(order < 2, order + 2, 3 - order)
+        rel = lax.rem(it + 1, 4)
+        grp = jnp.where(order < 2, 1, 0)
+
+        for at, event, n in ((4, send_core, 2), (6, send_x, 2), (8, send_core, 3), (10, send_x, 3)):
+
+            @pl.when((it == at) & has_prev)
+            def _(event=event, n=n):
+                event(n)
+
+        @pl.when(it == 12)
+        def _():
+            send_core(1)
+
+        @pl.when(it == 14)
+        def _():
+            send_x(1)
+
+        at = pl.ds(pl.multiple_of(seg * SEG, SEG), SEG)
+        keys, vals = kvg[0, at, :], kvg[1, at, :]
+        dv = jnp.dot(dot[grp, rel], e_buf[seg, rel], preferred_element_type=F32)
+        dk = None
+        for h in range(NH):
+            r = hrows[h]
+            dp = lax.dot_general(doraw[rel, :, hcols[h]], vals, NT, preferred_element_type=F32)
+            parts = []
+            for g0 in range(0, SET, VR):
+                g = slice(h * SET + g0, h * SET + g0 + VR)
+                d = st_d[rel, g, :]
+                part = []
+                for j in range(nl):
+                    e = e_buf[seg, rel, g, lanes(j)].astype(F32)
+                    part.append((e * (dp[g0 : g0 + VR, lanes(j)] - d)).astype(BF16))
+                parts.append(jnp.concatenate(part, axis=1))
+            ds = jnp.concatenate(parts, axis=0)
+            dqp[rel, r, :] += jnp.dot(ds, keys, preferred_element_type=F32) * (wgt[grp, rel, r, :] * SCALE)
+            part = jnp.dot(qt[grp, rel, :, r], ds, preferred_element_type=F32)
+            dk = part if dk is None else dk + part
+        for j in range(nl):
+            dva[seg * nl + j] += dv[:, lanes(j)]
+            dka[seg * nl + j] += dk[:, lanes(j)]
+
+        @pl.when(seg == 0)
+        def _():
+            for h in range(NH):
+                dqs[rel, :, hcols[h]] = dqp[rel, hrows[h], :].astype(BF16)
+
+            @pl.when(rel > 0)
             def _():
-                take_previous()
-
-            for half in range(2):
-                b = pair * 2 + half
-                keys = kvg[0, pl.ds(pl.multiple_of(b * SEG, SEG), SEG), :]
-                for h in range(NH):
-                    r = slice(h * SET, h * SET + SET)
-                    s = lax.dot_general(
-                        qraw[rel, :, h * HEAD : h * HEAD + HEAD], keys, NT, preferred_element_type=F32
-                    )
-                    m = mx[r, :]
-                    for j in range(nl):
-                        at = slice(j * 128, j * 128 + 128)
-                        sj = jnp.where(pk[b * nl + j, 0:1, :] <= pq[rel], s[:, at], MASKED)
-                        m = jnp.maximum(m, sj)
-                        s_buf[b, r, at] = sj
-                    mx[r, :] = m
-            return 0
-
-        lax.fori_loop(0, npair, scores, 0)
-        for h in range(NH):
-            r = slice(h * SET, h * SET + SET)
-            mx[r, :] = jnp.broadcast_to(jnp.max(mx[r, :], axis=1, keepdims=True) * SCALE2, (SET, 128))
-        ls[...] = jnp.zeros_like(ls)
-        dd[...] = jnp.zeros_like(dd)
-
-        def weights(pair, _):
-            for half in range(2):
-                b = pair * 2 + half
-                vals = kvg[1, pl.ds(pl.multiple_of(b * SEG, SEG), SEG), :]
-                for h in range(NH):
-                    dp = lax.dot_general(
-                        doraw[rel, :, h * HEAD : h * HEAD + HEAD], vals, NT, preferred_element_type=F32
-                    )
-                    for g0 in range(0, SET, VR):
-                        g = slice(h * SET + g0, h * SET + g0 + VR)
-                        m, l, d = mx[g, :], ls[g, :], dd[g, :]
-                        for j in range(nl):
-                            at = slice(j * 128, j * 128 + 128)
-                            e = jnp.exp2(s_buf[b, g, at] * SCALE2 - m)
-                            dpj = dp[g0 : g0 + VR, at]
-                            l = l + e
-                            d = d + e * dpj
-                            e_buf[b, g, at] = e.astype(BF16)
-                            dp_buf[b, g, at] = dpj
-                        ls[g, :] = l
-                        dd[g, :] = d
-            return 0
-
-        lax.fori_loop(0, npair, weights, 0)
-        for h in range(NH):
-            r = slice(h * SET, h * SET + SET)
-            rinv = 1.0 / jnp.sum(ls[r, :], axis=1, keepdims=True)
-            delta = jnp.sum(dd[r, :], axis=1, keepdims=True) * rinv
-            ls[r, :] = jnp.broadcast_to(rinv, (SET, 128))
-            dd[r, :] = jnp.broadcast_to(delta, (SET, 128))
-            hc = slice(h * HEAD, h * HEAD + HEAD)
-            qt[:, r] = (qraw[rel, :, hc].astype(F32) * rinv).astype(BF16).T
-            dot[:, r] = (doraw[rel, :, hc].astype(F32) * rinv).astype(BF16).T
-        dqa[...] = jnp.zeros_like(dqa)
-
-        def grads(step, _):
-            pair = npair - 1 - step
-            for half in range(2):
-                b = pair * 2 + half
-                keys = kvg[0, pl.ds(pl.multiple_of(b * SEG, SEG), SEG), :]
-                dv = jnp.dot(dot[...], e_buf[b], preferred_element_type=F32)
-                dk = None
-                for h in range(NH):
-                    r = slice(h * SET, h * SET + SET)
-                    parts = []
-                    for g0 in range(0, SET, VR):
-                        g = slice(h * SET + g0, h * SET + g0 + VR)
-                        d = dd[g, :]
-                        part = []
-                        for j in range(nl):
-                            at = slice(j * 128, j * 128 + 128)
-                            part.append((e_buf[b, g, at].astype(F32) * (dp_buf[b, g, at] - d)).astype(BF16))
-                        parts.append(jnp.concatenate(part, axis=1))
-                    ds = jnp.concatenate(parts, axis=0)
-                    dqa[r, :] += jnp.dot(ds, keys, preferred_element_type=F32)
-                    part = jnp.dot(qt[:, r], ds, preferred_element_type=F32)
-                    dk = part if dk is None else dk + part
-                for j in range(nl):
-                    blk = b * nl + j
-                    dva[blk] += dv[:, j * 128 : j * 128 + 128]
-                    dka[blk] += dk[:, j * 128 : j * 128 + 128]
-
-            @pl.when((rel == 3) & (pair == 1))
+                dq_copy(rel, 0).start()
+
+            @pl.when(rel == 0)
             def _():
-                send_core(2)
-                send_core(3)
-
-            return 0
-
-        lax.fori_loop(0, npair, grads, 0)
-        for h in range(NH):
-            r = slice(h * SET, h * SET + SET)
-            dqs[rel, :, h * HEAD : h * HEAD + HEAD] = (dqa[r, :] * (ls[r, :] * SCALE)).astype(BF16)
-
-        @pl.when(rel > 0)
-        def _():
-            dq_copy(rel, 0).start()
-
-        @pl.when(rel == 0)
-        def _():
-            dq_local.start()
-
-        dq_copy(rel, 1).start()
+                dq_local.start()
+
+            dq_copy(rel, 1).start()
+
         return 0
 
-    lax.fori_loop(0, 4, row_set, 0)
-
-    send_core(1)
+    lax.fori_loop(jnp.where(has_prev, 0, 8), 16, gradients, 0)
     send_core(0)
-
-    @pl.when(has_prev)
-    def _():
-        send_x(2)
-        send_x(3)
-
-    send_x(1)
     rc_copy(0).wait_recv()
 
     def own(yy, _):
@@ -457,6 +504,7 @@
 
 def on_device(queries, keys, values, output_gradient, span_order):
     vmem = pl.BlockSpec(memory_space=pltpu.VMEM)
+    hbm = pl.BlockSpec(memory_space=pl.ANY)
     dma = pltpu.SemaphoreType.DMA
     return pl.pallas_call(
         kernel,
@@ -465,23 +513,23 @@
             jax.ShapeDtypeStruct(keys.shape, BF16),
             jax.ShapeDtypeStruct(values.shape, BF16),
         ],
-        in_specs=[vmem, vmem, vmem, vmem, pl.BlockSpec(memory_space=pltpu.SMEM)],
-        out_specs=[vmem, vmem, vmem],
+        in_specs=[hbm, vmem, vmem, hbm, pl.BlockSpec(memory_space=pltpu.SMEM)],
+        out_specs=[hbm, vmem, vmem],
         scratch_shapes=[
             pltpu.VMEM((4, SET, COLS), BF16),
             pltpu.VMEM((4, SET, COLS), BF16),
             pltpu.VMEM((2, NKEY, HEAD), BF16),
             pltpu.VMEM((32, 8, TOK), F32),
             pltpu.VMEM((4, SET, 128), F32),
-            pltpu.VMEM((HEAD, ROWS), BF16),
-            pltpu.VMEM((HEAD, ROWS), BF16),
-            pltpu.VMEM((4, ROWS, SEG), F32),
-            pltpu.VMEM((4, ROWS, SEG), F32),
-            pltpu.VMEM((4, ROWS, SEG), BF16),
+            pltpu.VMEM((2, 4, HEAD, ROWS), BF16),
+            pltpu.VMEM((2, 4, HEAD, ROWS), BF16),
+            pltpu.VMEM((2, ROWS, SEG), F32),
+            pltpu.VMEM((4, 4, ROWS, SEG), BF16),
             pltpu.VMEM((ROWS, 128), F32),
-            pltpu.VMEM((ROWS, 128), F32),
-            pltpu.VMEM((ROWS, 128), F32),
-            pltpu.VMEM((ROWS, HEAD), F32),
+            pltpu.VMEM((2, 4, ROWS, 128), F32),
+            pltpu.VMEM((4, ROWS, 128), F32),
+            pltpu.VMEM((4, ROWS, 128), F32),
+            pltpu.VMEM((4, ROWS, HEAD), F32),
             pltpu.VMEM((32, HEAD, 128), F32),
             pltpu.VMEM((32, HEAD, 128), F32),
             pltpu.VMEM((4, SET, COLS), BF16),
@@ -502,7 +550,7 @@
             dma((3,)), dma((3,)),
         ],
         compiler_params=pltpu.CompilerParams(
-            collective_id=0, has_side_effects=True, vmem_limit_bytes=60 * 2**20
+            collective_id=0, has_side_effects=True, vmem_limit_bytes=62 * 2**20
         ),
         name="attention_backward",
     )(queries, keys, values, output_gradient, span_order)

time: 89.2 us -> 80.9 us (0.907)
  the two profiles are of different devices: /device:TPU:1 before, /device:TPU:34 now
where the time goes in v3:
time: 80.9 us; the launch traced here: 80.7 us
  Pallas kernels  76.4 us (94%)
  local copies, waits for them, and re-layouts  3.71 us (5%)
    pallas_call x1, Pallas kernels, on_device(): pl.pallas_call(kernel, out_shape=[jax.ShapeDtypeStruct(queries.shape, BF1...  76.4 us
    unnamed x7, local copies, waits for them, and re-layouts  3.71 us

profile of v3, /device:TPU:34, one launch (start us, length us, event | category | flops | bytes accessed | tf_op | source)
XLA Modules:
  0.0 80.7 jit_solution(4498904450920982326)
XLA Ops:
  0.6 76.4 %attention_backward.1 = (bf16[128,3072]{1,0:T(8,128)(2,1)}, bf16[128,512]{1,0:T(8,128)(2,1)}, bf16[128,512]{1,0:T(8,128)(2,1)}) custom-call(bf16[128,3072]{1,0:T(8,128)(2,1)} %q_ref.1, bf16[128,512]{1,0:T(8,128)(2,1)} %k_ref.1, bf16[128,512]{1,0:T(8,128)(2,1)} %v_ref.1, bf16[128,3072]{1,0:T(8,128)(2,1)} %do_ref.1, s32[32]{0:T(128)} %span_ref.1), custom_call_target="tpu_custom_call" | custom-call | tf_op jit(solution)/shard_map/attention_backward/pallas_call | solution.py:509
  77.0 0.0 copy-start.1
  77.0 2.1 %copy.11 = bf16[128,3072]{1,0:T(8,128)(2,1)} copy(bf16[128,3072]{1,0:T(8,128)(2,1)} %get-tuple-element.6) | data formatting | bytes 1572864
  79.1 0.0 copy-done.1
  79.1 0.0 copy-start
  79.1 0.7 copy.12
  79.8 0.3 copy-done
  80.1 0.7 copy.13
Async XLA Ops:
  77.0 2.1 %copy-start.1 = (bf16[128,512]{1,0:T(8,128)(2,1)S(1)}, bf16[128,512]{1,0:T(8,128)(2,1)}, u32[]{:S(2)}) copy-start(bf16[128,512]{1,0:T(8,128)(2,1)} %get-tuple-element.7) | copy-start | bytes 393220
  79.1 1.0 %copy-start = (bf16[128,512]{1,0:T(8,128)(2,1)S(1)}, bf16[128,512]{1,0:T(8,128)(2,1)}, u32[]{:S(2)}) copy-start(bf16[128,512]{1,0:T(8,128)(2,1)} %get-tuple-element.8) | copy-start | bytes 393220

commit v4 on v3

--- a/solution.py
+++ b/solution.py
@@ -502,11 +502,17 @@
             rx_copy(seg - 1).wait_send()
 
 
+def hand_over(a0, a1, a2, b0, b1, b2):
+    b0[...] = a0[...]
+    b1[...] = a1[...]
+    b2[...] = a2[...]
+
+
 def on_device(queries, keys, values, output_gradient, span_order):
     vmem = pl.BlockSpec(memory_space=pltpu.VMEM)
     hbm = pl.BlockSpec(memory_space=pl.ANY)
     dma = pltpu.SemaphoreType.DMA
-    return pl.pallas_call(
+    results = pl.pallas_call(
         kernel,
         out_shape=[
             jax.ShapeDtypeStruct(queries.shape, BF16),
@@ -554,6 +560,17 @@
         ),
         name="attention_backward",
     )(queries, keys, values, output_gradient, span_order)
+    parts = 2
+    blocks = [pl.BlockSpec((x.shape[0] // parts, x.shape[1]), lambda n: (n, 0)) for x in results]
+    return pl.pallas_call(
+        hand_over,
+        grid=(parts,),
+        out_shape=[jax.ShapeDtypeStruct(x.shape, BF16) for x in results],
+        in_specs=blocks,
+        out_specs=blocks,
+        compiler_params=pltpu.CompilerParams(vmem_limit_bytes=62 * 2**20),
+        name="hand_over",
+    )(*results)
 
 
 def solution(mesh):

time: 80.9 us -> 79.2 us (0.979)
  local copies, waits for them, and re-layouts: 3.71 us -> 0 us
  Pallas kernels: 76.4 us -> 78.4 us
    unnamed x7 -> x0, local copies, waits for them, and re-layouts: 3.71 us -> none
    pallas_call x0 -> x1, Pallas kernels: none -> 2.04 us  [on_device(): pl.pallas_call(hand_over, grid=(parts,), out_shape=[jax.ShapeDtypeStruct(...]
where the time goes in v4:
time: 79.2 us; the launch traced here: 79 us
  Pallas kernels  78.4 us (99%)
    pallas_call x1, Pallas kernels, on_device(): pl.pallas_call(kernel, out_shape=[jax.ShapeDtypeStruct(queries.shape, BF1...  76.4 us
    pallas_call x1, Pallas kernels, on_device(): pl.pallas_call(hand_over, grid=(parts,), out_shape=[jax.ShapeDtypeStruct(...  2.04 us

profile of v4, /device:TPU:34, one launch (start us, length us, event | category | flops | bytes accessed | tf_op | source)
XLA Modules:
  0.0 79.0 jit_solution(11273003327233005167)
XLA Ops:
  0.6 76.4 %attention_backward.1 = (bf16[128,3072]{1,0:T(8,128)(2,1)}, bf16[128,512]{1,0:T(8,128)(2,1)}, bf16[128,512]{1,0:T(8,128)(2,1)}) custom-call(bf16[128,3072]{1,0:T(8,128)(2,1)} %q_ref.1, bf16[128,512]{1,0:T(8,128)(2,1)} %k_ref.1, bf16[128,512]{1,0:T(8,128)(2,1)} %v_ref.1, bf16[128,3072]{1,0:T(8,128)(2,1)} %do_ref.1, s32[32]{0:T(128)} %span_ref.1), custom_call_target="tpu_custom_call" | custom-call | tf_op jit(solution)/shard_map/attention_backward/pallas_call | solution.py:515
  77.0 2.0 %hand_over.1 = (bf16[128,3072]{1,0:T(8,128)(2,1)}, bf16[128,512]{1,0:T(8,128)(2,1)}, bf16[128,512]{1,0:T(8,128)(2,1)}) custom-call(bf16[128,3072]{1,0:T(8,128)(2,1)} %get-tuple-element.6.a0, bf16[128,512]{1,0:T(8,128)(2,1)} %get-tuple-element.7.a1, bf16[128,512]{1,0:T(8,128)(2,1)} %get-tuple-element.8.a2), custom_call_target="tpu_custom_call" | custom-call | tf_op jit(solution)/shard_map/hand_over/pallas_call | solution.py:565

commit v5 on v4

--- a/solution.py
+++ b/solution.py
@@ -381,7 +381,6 @@
 
         at = pl.ds(pl.multiple_of(seg * SEG, SEG), SEG)
         keys, vals = kvg[0, at, :], kvg[1, at, :]
-        dv = jnp.dot(dot[grp, rel], e_buf[seg, rel], preferred_element_type=F32)
         dk = None
         for h in range(NH):
             r = hrows[h]
@@ -399,6 +398,7 @@
             dqp[rel, r, :] += jnp.dot(ds, keys, preferred_element_type=F32) * (wgt[grp, rel, r, :] * SCALE)
             part = jnp.dot(qt[grp, rel, :, r], ds, preferred_element_type=F32)
             dk = part if dk is None else dk + part
+        dv = jnp.dot(dot[grp, rel], e_buf[seg, rel], preferred_element_type=F32)
         for j in range(nl):
             dva[seg * nl + j] += dv[:, lanes(j)]
             dka[seg * nl + j] += dk[:, lanes(j)]

time: 79.2 us -> 78.9 us (level)
  no operation moved by 1% of the time
where the time goes in v5:
time: 78.9 us; the launch traced here: 78.8 us
  Pallas kernels  78.1 us (99%)
    pallas_call x1, Pallas kernels, on_device(): pl.pallas_call(kernel, out_shape=[jax.ShapeDtypeStruct(queries.shape, BF1...  76.1 us
    pallas_call x1, Pallas kernels, on_device(): pl.pallas_call(hand_over, grid=(parts,), out_shape=[jax.ShapeDtypeStruct(...  2.04 us

profile of v5, /device:TPU:34, one launch (start us, length us, event | category | flops | bytes accessed | tf_op | source)
XLA Modules:
  0.0 78.8 jit_solution(3840026527602856295)
XLA Ops:
  0.6 76.1 %attention_backward.1 = (bf16[128,3072]{1,0:T(8,128)(2,1)}, bf16[128,512]{1,0:T(8,128)(2,1)}, bf16[128,512]{1,0:T(8,128)(2,1)}) custom-call(bf16[128,3072]{1,0:T(8,128)(2,1)} %q_ref.1, bf16[128,512]{1,0:T(8,128)(2,1)} %k_ref.1, bf16[128,512]{1,0:T(8,128)(2,1)} %v_ref.1, bf16[128,3072]{1,0:T(8,128)(2,1)} %do_ref.1, s32[32]{0:T(128)} %span_ref.1), custom_call_target="tpu_custom_call" | custom-call | tf_op jit(solution)/shard_map/attention_backward/pallas_call | solution.py:515
  76.7 2.0 %hand_over.1 = (bf16[128,3072]{1,0:T(8,128)(2,1)}, bf16[128,512]{1,0:T(8,128)(2,1)}, bf16[128,512]{1,0:T(8,128)(2,1)}) custom-call(bf16[128,3072]{1,0:T(8,128)(2,1)} %get-tuple-element.6.a0, bf16[128,512]{1,0:T(8,128)(2,1)} %get-tuple-element.7.a1, bf16[128,512]{1,0:T(8,128)(2,1)} %get-tuple-element.8.a2), custom_call_target="tpu_custom_call" | custom-call | tf_op jit(solution)/shard_map/hand_over/pallas_call | solution.py:565
